TPU v7x, 32 devices: a whole 2x2x4 slice. The times are simulated.
32 devices in a mesh: groups: 2 (over y), dp: 4 (over z), tensor: 2 (over x), seq: 2 (over core).
Axes of the slice: x: 2, y: 2, z: 4, core: 2. Of those that a mesh axis runs over, the one named last changes fastest.
Arguments:
- activations: bfloat16 [8, 512, 4096], P(('groups', 'dp'), 'seq', 'tensor'), parts along dimension 0, may hold values from -6 to 6
- gate_input: bfloat16 [8, 512, 7168], P(('groups', 'dp'), None, ('tensor', 'seq')), parts along dimension 0, may hold values from -8 to 8
- out_grad: bfloat16 [8, 512, 4096], P(('groups', 'dp'), 'seq'), parts along dimension 0, may hold values from -6 to 6
- down_weight: bfloat16 [7168, 4096], P(('tensor', 'seq')), may hold values from -0.0625 to 0.0625
- proj_in: bfloat16 [4096, 64], P('tensor'), may hold values from -0.09375 to 0.09375
- proj_out: bfloat16 [7168, 64], P(('tensor', 'seq')), may hold values from -0.125 to 0.125
- precond_in: float32 [64, 64], replicated, may hold values from -1 to 2, as said below
- precond_out: float32 [64, 64], replicated, may hold values from -1 to 2, as said below
- queries: float32 [128, 4096], P(('groups', 'dp')), parts along dimension 0, may hold values from -6 to 6
Outputs:
- scores: float32 [8, 64], P(('groups', 'dp')), parts along dimension 0
There are 2 independent parts, one for each index of `groups`. A program takes and returns all parts, laid end to end along the dimension named above; an argument that names none is the same for every part. Nothing has to cross between parts.
Inputs may be any that keep to these rules, and one draw needn't show every extreme that they name: `precond_in`: symmetric. `precond_out`: symmetric.
All inputs are finite; a program needn't handle non-finite values.
Results may differ from a plain program's by a relative error of at most 0.0028.
Values may be sent and summed in bfloat16 or wider, within the bound.
A program may use at most 64 MiB of HBM per device.

v0:
```python
import math

import jax
import jax.numpy as jnp
from jax import lax
from jax.sharding import PartitionSpec as P


def body(
    activations,
    gate_input,
    out_grad,
    down_weight,
    proj_in,
    proj_out,
    precond_in,
    precond_out,
    queries,
):
    shard_piece = lax.all_gather(out_grad, "seq", axis=1, tiled=True)
    count = shard_piece.shape[1]
    flat_grad = shard_piece.reshape(-1, shard_piece.shape[2])
    hid_grad = lax.dot_general(
        flat_grad, down_weight, (((1,), (1,)), ((), ())), preferred_element_type=jnp.float32
    )
    gate_flat = gate_input.reshape(-1, gate_input.shape[2]).astype(jnp.float32)
    up_grad = (hid_grad * jax.nn.silu(gate_flat)).astype(jnp.bfloat16)
    projected = jnp.dot(up_grad, proj_out, preferred_element_type=jnp.float32)
    right_terms = projected.reshape(shard_piece.shape[0], count, -1)
    right_local = lax.psum_scatter(right_terms, "seq", scatter_dimension=1, tiled=True)
    act_flat = activations.reshape(-1, activations.shape[2])
    left_terms = jnp.dot(act_flat, proj_in, preferred_element_type=jnp.float32).reshape(
        activations.shape[0], activations.shape[1], -1
    )
    left_factor, right_factor = lax.psum((left_terms, right_local), "tensor")
    local_grads = jnp.einsum(
        "etk,etl->ekl", left_factor, right_factor, precision=lax.Precision.HIGHEST
    )
    example_grads = lax.psum(local_grads, "seq")
    section_one = jnp.einsum(
        "ik,ekl->eil", precond_in, example_grads, precision=lax.Precision.HIGHEST
    )
    precond_grads = jnp.einsum(
        "eil,lj->eij", section_one, precond_out, precision=lax.Precision.HIGHEST
    )
    flattened = precond_grads.reshape(precond_grads.shape[0], -1)
    score_scale = 1.0 / math.sqrt(gate_input.shape[1] * precond_in.shape[0] * precond_out.shape[0])
    return (
        jnp.dot(
            flattened,
            lax.all_gather(queries, "dp", axis=0, tiled=True).T,
            precision=lax.Precision.HIGHEST,
        )
        * score_scale
    )


def solution(mesh):
    return jax.shard_map(
        body,
        mesh=mesh,
        in_specs=(
            P(("groups", "dp"), "seq", "tensor"),
            P(("groups", "dp"), None, ("tensor", "seq")),
            P(("groups", "dp"), "seq", None),
            P(("tensor", "seq"), None),
            P("tensor", None),
            P(("tensor", "seq"), None),
            P(),
            P(),
            P(("groups", "dp"), None),
        ),
        out_specs=P(("groups", "dp"), None),
        check_vma=False,
    )
```

profile of v0, /device:TPU:0, one launch (start us, length us, event | category | flops | bytes accessed | tf_op | source)
XLA Modules:
  0.0 92.6 jit_solution(10706504667145099145)
XLA Ops:
  7.4 0.0 copy-start
  7.4 0.0 all-gather.3.cloned.1.call-start
  7.4 0.7 all-gather.3.cloned.1.call-update
  8.1 0.0 copy-start.1
  8.1 0.0 copy-start.2
  8.1 0.0 copy-start.3
  8.1 0.0 reduce-scatter.2.cloned.1.call-start
  8.2 18.0 %all-gather.3.cloned.1.call-done = bf16[1,512,4096]{2,1,0:T(8,128)(2,1)} async-done(((bf16[1,256,4096]{2,1,0:T(8,128)(2,1)}), bf16[1,512,4096]{2,1,0:T(8,128)(2,1)}) %all-gather.3.cloned.1.call-update) | async-done | bytes 4194320 | tf_op jit(solution)/shard_map/all_gather | solution.py:20
  26.1 16.5 %fusion.14 = f32[1,512,64]{1,2,0:T(8,128)} fusion(bf16[1792,64]{0,1:T(8,128)(2,1)} %param.14, bf16[1792,4096]{1,0:T(8,128)(2,1)} %param.12, bf16[1,512,4096]{2,1,0:T(8,128)(2,1)} %all-gather.3.cloned.1.call-done, bf16[1,512,1792]{2,1,0:T(8,128)(2,1)} %param.10), kind=kOutput, calls=%fused_computation.12 | convolution fusion | flops 7640055808 | bytes 21069824 | tf_op jit(solution)/shard_map/dot_general | solution.py:28
  42.6 0.0 reduce-scatter.2.cloned.1.call-update
  42.6 0.0 all-reduce.3.cloned.1.call-start
  42.7 0.0 copy-done
  42.7 0.0 copy-done.1
  42.7 1.1 %fusion.19 = f32[256,64]{1,0:T(8,128)} fusion(bf16[2048,64]{0,1:T(8,128)(2,1)S(1)} %copy-done.1, bf16[1,256,2048]{2,1,0:T(8,128)(2,1)S(1)} %copy-done), kind=kOutput, calls=%fused_computation.17 | convolution fusion | flops 67108864 | bytes 1376256 | tf_op jit(solution)/shard_map/dot_general | solution.py:32
  43.8 7.7 %reduce-scatter.2.cloned.1.call-done = f32[1,256,64]{1,2,0:T(8,128)} async-done(((f32[1,512,64]{1,2,0:T(8,128)}), f32[1,256,64]{1,2,0:T(8,128)}) %reduce-scatter.2.cloned.1.call-update) | async-done | bytes 65552 | tf_op jit(solution)/shard_map/reduce_scatter | solution.py:30
  51.4 0.0 all-reduce.3.cloned.1.call-update
  51.5 0.0 all-gather.5.cloned.1.call-start
  51.5 0.5 all-gather.5.cloned.1.call-update
  52.0 25.5 %all-reduce.3.cloned.1.call-done = (f32[256,64]{1,0:T(8,128)}, f32[256,64]{0,1:T(8,128)}) async-done(((f32[256,64]{1,0:T(8,128)}, f32[256,64]{0,1:T(8,128)}), (f32[256,64]{1,0:T(8,128)}, f32[256,64]{0,1:T(8,128)})) %all-reduce.3.cloned.1.call-update) | async-done | bytes 131088 | tf_op jit(solution)/shard_map/psum | solution.py:35
  77.5 1.3 %fusion.22 = f32[64,64]{1,0:T(8,128)S(1)} fusion(f32[256,64]{1,0:T(8,128)} %get-tuple-element.5, f32[256,64]{0,1:T(8,128)} %get-tuple-element.6), kind=kOutput, calls=%fused_computation.20 | convolution fusion | flops 12582912 | bytes 147456 | tf_op jit(solution)/shard_map/etk,etl->ekl/dot_general | solution.py:36
  78.8 3.4 %psum.23 = f32[64,64]{1,0:T(8,128)S(1)} all-reduce(f32[64,64]{1,0:T(8,128)S(1)} %fusion.22), channel_id=1, replica_groups=mesh['groups'=2,'dp'=4,'tensor'=2,'seq'=2] {'seq'}, use_global_device_ids=true, to_apply=%region_3.4 | all-reduce | flops 4096 | bytes 32768 | tf_op jit(solution)/shard_map/psum | solution.py:39
  82.2 0.0 copy-done.2
  82.2 0.2 convolution_bitcast_fusion
  82.5 0.0 copy-done.3
  82.5 0.2 fusion.23
  82.7 0.1 reshape.50
  82.8 0.0 all-gather.5.cloned.1.call-done
  82.8 2.7 %fusion.18 = f32[1,64]{1,0:T(1,128)} fusion(f32[4096,1]{0,1:T(1,128)S(1)} %reshape.50, f32[64,4096]{1,0:T(8,128)} %all-gather.5.cloned.1.call-done), kind=kOutput, calls=%fused_computation.16 | convolution fusion | flops 3145792 | bytes 1065216 | tf_op jit(solution)/shard_map/dot_general | solution.py:49
Async XLA Ops:
  7.4 35.3 %copy-start = (bf16[1,256,2048]{2,1,0:T(8,128)(2,1)S(1)}, bf16[1,256,2048]{2,1,0:T(8,128)(2,1)}, u32[]{:S(2)}) copy-start(bf16[1,256,2048]{2,1,0:T(8,128)(2,1)} %param.9) | copy-start | bytes 3145732
  7.4 18.8 %all-gather.3.cloned.1.call-start = ((), (), s32[]{:S(2)}) async-start(), calls=%async_computation.1 | async-start | bytes 6291456 | tf_op jit(solution)/shard_map/all_gather | solution.py:20
  8.1 34.6 %copy-start.1 = (bf16[2048,64]{0,1:T(8,128)(2,1)S(1)}, bf16[2048,64]{0,1:T(8,128)(2,1)}, u32[]{:S(2)}) copy-start(bf16[2048,64]{0,1:T(8,128)(2,1)} %param.13) | copy-start | bytes 786436
  8.1 74.1 %copy-start.2 = (f32[64,64]{1,0:T(8,128)S(1)}, f32[64,64]{1,0:T(8,128)}, u32[]{:S(2)}) copy-start(f32[64,64]{1,0:T(8,128)} %param.15) | copy-start | bytes 49156
  8.1 74.4 %copy-start.3 = (f32[64,64]{1,0:T(8,128)S(1)}, f32[64,64]{1,0:T(8,128)}, u32[]{:S(2)}) copy-start(f32[64,64]{1,0:T(8,128)} %param.16) | copy-start | bytes 49156
  8.1 43.3 %reduce-scatter.2.cloned.1.call-start = ((), (), s32[]{:S(2)}) async-start(), calls=%async_computation.2 | async-start | bytes 196608 | tf_op jit(solution)/shard_map/reduce_scatter | solution.py:30
  42.6 34.9 %all-reduce.3.cloned.1.call-start = ((), (), s32[]{:S(2)}) async-start(), calls=%async_computation.4 | async-start | bytes 393216 | tf_op jit(solution)/shard_map/psum | solution.py:35
  51.5 31.4 %all-gather.5.cloned.1.call-start = ((), (), s32[]{:S(2)}) async-start(), calls=%async_computation.3 | async-start | bytes 1310720 | tf_op jit(solution)/shard_map/all_gather | solution.py:51
Sparse Core Ops, SparseCore 0:
  9.7 16.3 all-gather.2
  42.8 8.6 reduce-scatter.1
  53.8 23.6 all-reduce.2
Sparse Core Ops, SparseCore 1:
  53.5 29.1 all-gather.4
where the time goes:
time: 92.8 us; the launch traced here: 92.6 us
  waiting for transfers between devices  52.4 us (56%)
  matrix products  22 us (24%)
  between operations  14.6 us (16%)
  blocking collectives  3.41 us (4%)
    psum x1, waiting for transfers between devices, body(): left_factor, right_factor = lax.psum((left_terms, right_local), 'tensor')  25.5 us
    all_gather x1, waiting for transfers between devices, body(): shard_piece = lax.all_gather(out_grad, 'seq', axis=1, tiled=True)  18 us
    dot_general x1, matrix products, body(): projected = jnp.dot(up_grad, proj_out, preferred_element_type=jnp.float32)  16.5 us
    reduce_scatter x1, waiting for transfers between devices, body(): lax.psum_scatter(right_terms, 'seq', scatter_dimension=1, tiled=True)  7.66 us
    psum x1, blocking collectives, body(): example_grads = lax.psum(local_grads, 'seq')  3.41 us
    dot_general x1, matrix products, body(): jnp.dot(flattened, lax.all_gather(queries, 'dp', axis=0, tiled=True).T, p...  2.67 us
  transfers between devices with their start and end apart: 4, of which 3 were waited for; matrix products, arithmetic and copies ran while one was open for 3% of the time, Pallas kernels for 0%

commit v1 on v0

v1 whole, which is shorter than its diff:
```python
import functools
import math

import jax
import jax.numpy as jnp
from jax import lax
from jax.experimental import pallas as pl
from jax.experimental.pallas import tpu as pltpu
from jax.sharding import PartitionSpec as P

MESH = pl.DeviceIdType.MESH
F32 = jnp.float32
BF16 = jnp.bfloat16
NT = (((1,), (1,)), ((), ()))
NN = (((1,), (0,)), ((), ()))


def split(x):
    hi = x.astype(BF16)
    return hi, (x - hi.astype(F32)).astype(BF16)


def kernel(
    dims, scale,
    act_h, gate_h, grad_h, down_h, pin_h, pout_h, cin_h, cout_h, query_h,
    out_ref,
    down, grad, gate, act, pin, pout, pout2, cin, cout, query, qsend, qall,
    lefts, rights, scores,
    down_sem, load_sem,
    grad_sem, left_send, left_recv, q_send, q_recv, qc_send, qc_recv, s_send, s_recv,
):
    groups, dp, tensor, seq, chunk = dims
    ff = down.shape[0]
    chunks = ff // chunk
    tokens = grad.shape[1]
    k1 = cin.shape[0]
    half = qsend.shape[1]
    nq_block = qsend.shape[0]
    ranks = tensor * seq
    g, z = lax.axis_index("groups"), lax.axis_index("dp")
    x, s = lax.axis_index("tensor"), lax.axis_index("seq")
    me = x * seq + s
    other = 1 - s

    def peer(k):
        r = lax.rem(me + k, ranks)
        return (g, z, r // seq, lax.rem(r, seq))

    def along(k):
        return (g, lax.rem(z + k, dp), x, s)

    barrier = pltpu.get_barrier_semaphore()
    for k in range(1, ranks):
        pl.semaphore_signal(barrier, inc=1, device_id=peer(k), device_id_type=MESH)
    for k in range(1, dp):
        pl.semaphore_signal(barrier, inc=1, device_id=along(k), device_id_type=MESH)

    def rows_of(c):
        return pl.ds(pl.multiple_of(c * chunk, chunk), chunk)

    def load(src, dst, i):
        copy = pltpu.make_async_copy(src, dst, load_sem.at[i])
        copy.start()
        return copy

    def down_copy(c):
        return pltpu.make_async_copy(
            down_h.at[rows_of(c)], down.at[rows_of(c)], down_sem.at[c]
        )

    def token_rows(b):
        return pl.ds(pl.multiple_of(b * tokens, tokens), tokens)

    get_query = load(query_h, query, 0)
    get_act = load(act_h.at[0], act, 1)
    get_pin = load(pin_h, pin, 2)
    get_cin = load(cin_h, cin, 3)
    get_cout = load(cout_h, cout, 4)
    get_pout = load(pout_h, pout, 5)
    get_grad = load(grad_h.at[0], grad.at[0], 6)
    get_gate0 = load(gate_h.at[0, token_rows(s)], gate.at[0], 7)
    for c in range(chunks):
        down_copy(c).start()
    get_gate1 = load(gate_h.at[0, token_rows(other)], gate.at[1], 8)

    pl.semaphore_wait(barrier, ranks - 1 + dp - 1)

    send_grad = pltpu.make_async_remote_copy(
        src_ref=grad_h.at[0], dst_ref=grad.at[1],
        send_sem=grad_sem.at[0], recv_sem=grad_sem.at[1],
        device_id=(g, z, x, other), device_id_type=MESH,
    )
    send_grad.start()

    get_query.wait()
    for h in range(seq):
        qall[z, h] = query[:, h * half:(h + 1) * half].astype(BF16)

    def q_copy(k, block):
        return pltpu.make_async_remote_copy(
            src_ref=qall.at[z, s], dst_ref=qall.at[block, s],
            send_sem=q_send.at[k], recv_sem=q_recv.at[block],
            device_id=along(k), device_id_type=MESH,
        )

    for k in range(1, dp):
        q_copy(k, z).start()

    get_act.wait()
    get_pin.wait()
    get_cin.wait()
    left = lax.dot_general(act[...], pin[...], NN, preferred_element_type=F32)
    cin_rows = jnp.concatenate(
        [cin[pl.ds(0, k1 // 2, 2), :], cin[pl.ds(1, k1 // 2, 2), :]], axis=0
    )
    lefts[me] = lax.dot_general(
        cin_rows, left, NT, precision=lax.Precision.HIGHEST, preferred_element_type=F32
    )

    def left_copy(k, rank):
        return pltpu.make_async_remote_copy(
            src_ref=lefts.at[me], dst_ref=lefts.at[rank],
            send_sem=left_send.at[k], recv_sem=left_recv.at[rank],
            device_id=peer(k), device_id_type=MESH,
        )

    for k in range(1, ranks):
        left_copy(k, me).start()

    get_cout.wait()
    get_pout.wait()
    cout2 = jnp.concatenate(split(cout[...]), axis=1)
    k2 = cout.shape[0]

    def project(c):
        y = lax.dot_general(pout[rows_of(c), :], cout2, NN, preferred_element_type=F32)
        pout2[rows_of(c), :] = jnp.concatenate(split(y[:, :k2] + y[:, k2:]), axis=1)

    def step(phase, c):
        hid = lax.dot_general(
            grad[phase], down[rows_of(c), :], NT, preferred_element_type=F32
        )
        v = gate[phase, :, rows_of(c)].astype(F32)
        up = (hid * (v / (1.0 + jnp.exp(-v)))).astype(BF16)
        rights[phase] += lax.dot_general(
            up, pout2[rows_of(c), :], NN, preferred_element_type=F32
        )

    rights[...] = jnp.zeros_like(rights)
    get_grad.wait()
    get_gate0.wait()

    @pl.loop(0, chunks)
    def _(c):
        project(c)
        down_copy(c).wait()
        step(0, c)

    get_gate1.wait()
    send_grad.wait()

    def qc_copy(block, owner):
        return pltpu.make_async_remote_copy(
            src_ref=qall.at[block, owner], dst_ref=qall.at[block, owner],
            send_sem=qc_send.at[block], recv_sem=qc_recv.at[block],
            device_id=(g, z, x, other), device_id_type=MESH,
        )

    for k in range(1, dp):
        block = lax.rem(z + dp - k, dp)
        q_copy(k, block).wait_recv()
        qc_copy(block, s).start()

    for k in range(1, ranks):
        left_copy(k, lax.rem(me + ranks - k, ranks)).wait_recv()

    @pl.loop(0, chunks)
    def _(c):
        step(1, c)

    def product(phase, block):
        total = lefts[block]
        for t in range(1, tensor):
            total = total + lefts[t * seq + block]
        l2 = jnp.concatenate(split(total), axis=0)
        r2 = jnp.concatenate(split(rights[phase]), axis=1)
        return lax.dot_general(l2, r2, NN, preferred_element_type=F32)

    m = product(0, s) + product(1, other)
    m = m[:k1] + m[k1:]
    m = m[:, :2 * k2] + m[:, 2 * k2:]
    m = (m[:, :k2] + m[:, k2:]) * scale
    wide = jnp.concatenate([m[:k1 // 2], m[k1 // 2:]], axis=1)

    for k in range(1, dp):
        block = lax.rem(z + dp - k, dp)
        qc_copy(block, other).wait_recv()

    lanes = 2 * k2
    rows = half // lanes
    sums = []
    for b in range(dp):
        acc = jnp.zeros((nq_block, lanes), F32)
        for h in range(seq):
            for r in range(rows):
                i = h * rows + r
                acc = acc + wide[i:i + 1, :] * qall[b, h, :, r * lanes:(r + 1) * lanes].astype(F32)
        sums.append(acc)
    acc = jnp.concatenate(sums, axis=0)
    row = jnp.sum(acc.T, axis=0, keepdims=True)
    scores[me] = jnp.broadcast_to(row, scores.shape[1:])

    def score_copy(k, rank):
        return pltpu.make_async_remote_copy(
            src_ref=scores.at[me], dst_ref=scores.at[rank],
            send_sem=s_send.at[k], recv_sem=s_recv.at[rank],
            device_id=peer(k), device_id_type=MESH,
        )

    for k in range(1, ranks):
        score_copy(k, me).start()
    for k in range(1, ranks):
        score_copy(k, lax.rem(me + ranks - k, ranks)).wait_recv()
    total = scores[0, 0:1]
    for r in range(1, ranks):
        total = total + scores[r, 0:1]
    out_ref[...] = total

    for k in range(1, ranks):
        score_copy(k, me).wait_send()
        left_copy(k, me).wait_send()
    for k in range(1, dp):
        q_copy(k, z).wait_send()
        qc_copy(lax.rem(z + dp - k, dp), s).wait_send()


def solution(mesh):
    shape = dict(mesh.shape)
    groups, dp, tensor, seq = (shape[a] for a in ("groups", "dp", "tensor", "seq"))

    def body(act, gate, grad, down, pin, pout, cin, cout, query):
        tokens, d_local = act.shape[1:]
        features = grad.shape[2]
        ff = down.shape[0]
        k1, k2 = pin.shape[1], pout.shape[1]
        nq_block, width = query.shape
        chunk = next(c for c in (256, 128) if ff % c == 0 and ff // c >= 4)
        chunks = ff // chunk
        ranks = tensor * seq
        nq = nq_block * dp
        scale = 1.0 / math.sqrt(gate.shape[1] * k1 * k2)
        dma = pltpu.SemaphoreType.DMA
        scratch = [
            pltpu.VMEM((ff, features), BF16),
            pltpu.VMEM((2, tokens, features), BF16),
            pltpu.VMEM((2, tokens, ff), BF16),
            pltpu.VMEM((tokens, d_local), BF16),
            pltpu.VMEM((d_local, k1), BF16),
            pltpu.VMEM((ff, k2), BF16),
            pltpu.VMEM((ff, 2 * k2), BF16),
            pltpu.VMEM((k1, k1), F32),
            pltpu.VMEM((k2, k2), F32),
            pltpu.VMEM((nq_block, width), F32),
            pltpu.VMEM((nq_block, width // seq), BF16),
            pltpu.VMEM((dp, seq, nq_block, width // seq), BF16),
            pltpu.VMEM((ranks, k1, tokens), F32),
            pltpu.VMEM((2, tokens, 2 * k2), F32),
            pltpu.VMEM((ranks, 8, nq), F32),
            dma((chunks,)),
            dma((9,)),
            dma((2,)),
            dma((ranks,)), dma((ranks,)),
            dma((dp,)), dma((dp,)),
            dma((dp,)), dma((dp,)),
            dma((ranks,)), dma((ranks,)),
        ]
        return pl.pallas_call(
            functools.partial(kernel, (groups, dp, tensor, seq, chunk), scale),
            out_shape=jax.ShapeDtypeStruct((1, nq), F32),
            in_specs=[pl.BlockSpec(memory_space=pl.ANY)] * 9,
            out_specs=pl.BlockSpec(memory_space=pltpu.VMEM),
            scratch_shapes=scratch,
            compiler_params=pltpu.CompilerParams(
                collective_id=0, has_side_effects=True, vmem_limit_bytes=58 * 2**20
            ),
            cost_estimate=pl.CostEstimate(
                flops=4 * tokens * ff * features,
                bytes_accessed=2 * ff * features,
                transcendentals=0,
            ),
        )(act, gate, grad, down, pin, pout, cin, cout, query)

    return jax.shard_map(
        body,
        mesh=mesh,
        in_specs=(
            P(("groups", "dp"), "seq", "tensor"),
            P(("groups", "dp"), None, ("tensor", "seq")),
            P(("groups", "dp"), "seq", None),
            P(("tensor", "seq"), None),
            P("tensor", None),
            P(("tensor", "seq"), None),
            P(),
            P(),
            P(("groups", "dp"), None),
        ),
        out_specs=P(("groups", "dp"), None),
        check_vma=False,
    )
```

time: 92.8 us -> 33.1 us (0.36)
  waiting for transfers between devices: 52.4 us -> 0 us
  Pallas kernels: 0 us -> 27.9 us
  matrix products: 22 us -> 0 us
  between operations: 14.6 us -> 0.01 us
  local copies, waits for them, and re-layouts: 0.1 us -> 5.04 us
  blocking collectives: 3.41 us -> 0 us
    pallas_call x0 -> x1, Pallas kernels: none -> 27.9 us  [body(): pl.pallas_call(functools.partial(kernel, (groups, dp, tensor, seq, chunk)...]
    psum x1 -> x0, waiting for transfers between devices: 25.5 us -> none  [body(): left_factor, right_factor = lax.psum((left_terms, right_local), 'tensor')]
    dot_general x6 -> x0, matrix products: 22 us -> none  [the longest x1 16.5 us: body(): projected = jnp.dot(up_grad, proj_out, preferred_element_type=jnp.float32)]
    all_gather x2 -> x0, waiting for transfers between devices: 18 us -> none  [the longest x1 18 us: body(): shard_piece = lax.all_gather(out_grad, 'seq', axis=1, tiled=True)]
    reduce_scatter x1 -> x0, waiting for transfers between devices: 7.66 us -> none  [body(): lax.psum_scatter(right_terms, 'seq', scatter_dimension=1, tiled=True)]
    unnamed x8 -> x3, local copies, waits for them, and re-layouts: 0.02 us -> 5.04 us
    psum x1 -> x0, blocking collectives: 3.41 us -> none  [body(): example_grads = lax.psum(local_grads, 'seq')]
    unnamed x4 -> x0, waiting for transfers between devices: 1.26 us -> none
  transfers between devices with their start and end apart: 4 -> 0, of which waited for: 3 -> 0; matrix products, arithmetic and copies ran while one was open for 3% -> 0% of each run, Pallas kernels for 0% -> 0%
where the time goes in v1:
time: 33.1 us; the launch traced here: 32.9 us
  Pallas kernels  27.9 us (84%)
  local copies, waits for them, and re-layouts  5.04 us (15%)
    pallas_call x1, Pallas kernels, body(): pl.pallas_call(functools.partial(kernel, (groups, dp, tensor, seq, chunk)...  27.9 us
    unnamed x3, local copies, waits for them, and re-layouts  5.04 us

profile of v1, /device:TPU:0, one launch (start us, length us, event | category | flops | bytes accessed | tf_op | source)
XLA Modules:
  0.0 32.9 jit_solution(1788855194825080188)
XLA Ops:
  0.0 1.9 %copy.11.pout_h = bf16[1792,64]{1,0:T(8,128)(2,1)} copy(bf16[1792,64]{0,1:T(8,128)(2,1)} %param.14) | data formatting | bytes 458752 | tf_op args[5]
  1.9 1.9 %copy.10.pin_h = bf16[2048,64]{1,0:T(8,128)(2,1)} copy(bf16[2048,64]{0,1:T(8,128)(2,1)} %param.13) | data formatting | bytes 524288 | tf_op args[4]
  3.9 27.9 %shard_map.91 = f32[1,64]{1,0:T(1,128)} custom-call(bf16[1,256,2048]{2,1,0:T(8,128)(2,1)} %act_h.1, bf16[1,512,1792]{2,1,0:T(8,128)(2,1)} %gate_h.1, bf16[1,256,4096]{2,1,0:T(8,128)(2,1)} %grad_h.1, bf16[1792,4096]{1,0:T(8,128)(2,1)} %down_h.1, bf16[2048,64]{1,0:T(8,128)(2,1)} %copy.10.pin_h, bf16[1792,64]{1,0:T(8,128)(2,1)} %copy.11.pout_h, ...), custom_call_target="tpu_custom_call" | custom-call | flops 7516192768 | bytes 14680064 | tf_op jit(solution)/shard_map/pallas_call | solution.py:277
  31.7 1.2 %copy.13 = f32[1,64]{1,0:T(1,128)} copy(f32[1,64]{1,0:T(1,128)} %shard_map.91) | data formatting | bytes 512

commit v2 on v1

--- a/solution.py
+++ b/solution.py
@@ -24,8 +24,8 @@
     dims, scale,
     act_h, gate_h, grad_h, down_h, pin_h, pout_h, cin_h, cout_h, query_h,
     out_ref,
-    down, grad, gate, act, pin, pout, pout2, cin, cout, query, qsend, qall,
-    lefts, rights, scores,
+    down, grad, gate, act, pin, pout, cin, cout, query, qall,
+    lefts, scores,
     down_sem, load_sem,
     grad_sem, left_send, left_recv, q_send, q_recv, qc_send, qc_recv, s_send, s_recv,
 ):
@@ -34,8 +34,8 @@
     chunks = ff // chunk
     tokens = grad.shape[1]
     k1 = cin.shape[0]
-    half = qsend.shape[1]
-    nq_block = qsend.shape[0]
+    nq_block = query.shape[0]
+    half = query.shape[1] // seq
     ranks = tensor * seq
     g, z = lax.axis_index("groups"), lax.axis_index("dp")
     x, s = lax.axis_index("tensor"), lax.axis_index("seq")
@@ -71,15 +71,16 @@
     def token_rows(b):
         return pl.ds(pl.multiple_of(b * tokens, tokens), tokens)
 
-    get_query = load(query_h, query, 0)
     get_act = load(act_h.at[0], act, 1)
     get_pin = load(pin_h, pin, 2)
+    get_query = load(query_h, query, 0)
     get_cin = load(cin_h, cin, 3)
     get_cout = load(cout_h, cout, 4)
     get_pout = load(pout_h, pout, 5)
     get_grad = load(grad_h.at[0], grad.at[0], 6)
+    down_copy(0).start()
     get_gate0 = load(gate_h.at[0, token_rows(s)], gate.at[0], 7)
-    for c in range(chunks):
+    for c in range(1, chunks):
         down_copy(c).start()
     get_gate1 = load(gate_h.at[0, token_rows(other)], gate.at[1], 8)
 
@@ -109,12 +110,12 @@
     get_act.wait()
     get_pin.wait()
     get_cin.wait()
-    left = lax.dot_general(act[...], pin[...], NN, preferred_element_type=F32)
+    left = lax.dot_general(pin[...], act[...], NT, preferred_element_type=F32)
     cin_rows = jnp.concatenate(
         [cin[pl.ds(0, k1 // 2, 2), :], cin[pl.ds(1, k1 // 2, 2), :]], axis=0
     )
     lefts[me] = lax.dot_general(
-        cin_rows, left, NT, precision=lax.Precision.HIGHEST, preferred_element_type=F32
+        cin_rows, left, NN, precision=lax.Precision.HIGHEST, preferred_element_type=F32
     )
 
     def left_copy(k, rank):
@@ -129,32 +130,24 @@
 
     get_cout.wait()
     get_pout.wait()
-    cout2 = jnp.concatenate(split(cout[...]), axis=1)
     k2 = cout.shape[0]
-
-    def project(c):
-        y = lax.dot_general(pout[rows_of(c), :], cout2, NN, preferred_element_type=F32)
-        pout2[rows_of(c), :] = jnp.concatenate(split(y[:, :k2] + y[:, k2:]), axis=1)
+    cout2 = jnp.concatenate(split(cout[...]), axis=0)
+    y = lax.dot_general(cout2, pout[...], NN, preferred_element_type=F32)
+    pout2 = jnp.concatenate(split(y[:k2] + y[k2:]), axis=0)
 
     def step(phase, c):
-        hid = lax.dot_general(
-            grad[phase], down[rows_of(c), :], NT, preferred_element_type=F32
-        )
-        v = gate[phase, :, rows_of(c)].astype(F32)
+        rows = slice(c * chunk, (c + 1) * chunk)
+        hid = lax.dot_general(down[rows, :], grad[phase], NT, preferred_element_type=F32)
+        v = gate[phase, :, rows].astype(F32).T
         up = (hid * (v / (1.0 + jnp.exp(-v)))).astype(BF16)
-        rights[phase] += lax.dot_general(
-            up, pout2[rows_of(c), :], NN, preferred_element_type=F32
-        )
-
-    rights[...] = jnp.zeros_like(rights)
+        return lax.dot_general(pout2[:, rows], up, NN, preferred_element_type=F32)
+
     get_grad.wait()
     get_gate0.wait()
-
-    @pl.loop(0, chunks)
-    def _(c):
-        project(c)
+    right0 = 0.0
+    for c in range(chunks):
         down_copy(c).wait()
-        step(0, c)
+        right0 = right0 + step(0, c)
 
     get_gate1.wait()
     send_grad.wait()
@@ -174,19 +167,19 @@
     for k in range(1, ranks):
         left_copy(k, lax.rem(me + ranks - k, ranks)).wait_recv()
 
-    @pl.loop(0, chunks)
-    def _(c):
-        step(1, c)
-
-    def product(phase, block):
+    def product(right, block):
         total = lefts[block]
-        for t in range(1, tensor):
-            total = total + lefts[t * seq + block]
+        for r in range(1, tensor):
+            total = total + lefts[r * seq + block]
         l2 = jnp.concatenate(split(total), axis=0)
-        r2 = jnp.concatenate(split(rights[phase]), axis=1)
-        return lax.dot_general(l2, r2, NN, preferred_element_type=F32)
-
-    m = product(0, s) + product(1, other)
+        r2 = jnp.concatenate(split(right), axis=0)
+        return lax.dot_general(l2, r2, NT, preferred_element_type=F32)
+
+    m = product(right0, s)
+    right1 = 0.0
+    for c in range(chunks):
+        right1 = right1 + step(1, c)
+    m = m + product(right1, other)
     m = m[:k1] + m[k1:]
     m = m[:, :2 * k2] + m[:, 2 * k2:]
     m = (m[:, :k2] + m[:, k2:]) * scale
@@ -242,9 +235,10 @@
         tokens, d_local = act.shape[1:]
         features = grad.shape[2]
         ff = down.shape[0]
-        k1, k2 = pin.shape[1], pout.shape[1]
+        pin, pout = pin.T, pout.T
+        k1, k2 = pin.shape[0], pout.shape[0]
         nq_block, width = query.shape
-        chunk = next(c for c in (256, 128) if ff % c == 0 and ff // c >= 4)
+        chunk = next(c for c in (896, 512, 256, 128) if ff % c == 0)
         chunks = ff // chunk
         ranks = tensor * seq
         nq = nq_block * dp
@@ -255,16 +249,13 @@
             pltpu.VMEM((2, tokens, features), BF16),
             pltpu.VMEM((2, tokens, ff), BF16),
             pltpu.VMEM((tokens, d_local), BF16),
-            pltpu.VMEM((d_local, k1), BF16),
-            pltpu.VMEM((ff, k2), BF16),
-            pltpu.VMEM((ff, 2 * k2), BF16),
+            pltpu.VMEM((k1, d_local), BF16),
+            pltpu.VMEM((k2, ff), BF16),
             pltpu.VMEM((k1, k1), F32),
             pltpu.VMEM((k2, k2), F32),
             pltpu.VMEM((nq_block, width), F32),
-            pltpu.VMEM((nq_block, width // seq), BF16),
             pltpu.VMEM((dp, seq, nq_block, width // seq), BF16),
             pltpu.VMEM((ranks, k1, tokens), F32),
-            pltpu.VMEM((2, tokens, 2 * k2), F32),
             pltpu.VMEM((ranks, 8, nq), F32),
             dma((chunks,)),
             dma((9,)),

time: 33.1 us -> 25.2 us (0.76)
  Pallas kernels: 27.9 us -> 23.9 us
  local copies, waits for them, and re-layouts: 5.04 us -> 1.19 us
    pallas_call x1, Pallas kernels: 27.9 us -> 23.9 us  [body(): pl.pallas_call(functools.partial(kernel, (groups, dp, tensor, seq, chunk)...]
    unnamed x3 -> x1, local copies, waits for them, and re-layouts: 5.04 us -> 1.19 us
where the time goes in v2:
time: 25.2 us; the launch traced here: 25.1 us
  Pallas kernels  23.9 us (95%)
  local copies, waits for them, and re-layouts  1.19 us (5%)
    pallas_call x1, Pallas kernels, body(): pl.pallas_call(functools.partial(kernel, (groups, dp, tensor, seq, chunk)...  23.9 us
    unnamed x1, local copies, waits for them, and re-layouts  1.19 us

profile of v2, /device:TPU:0, one launch (start us, length us, event | category | flops | bytes accessed | tf_op | source)
XLA Modules:
  0.0 25.1 jit_solution(4029397200860111187)
XLA Ops:
  0.0 23.9 %shard_map.91 = f32[1,64]{1,0:T(1,128)} custom-call(bf16[1,256,2048]{2,1,0:T(8,128)(2,1)} %act_h.1, bf16[1,512,1792]{2,1,0:T(8,128)(2,1)} %gate_h.1, bf16[1,256,4096]{2,1,0:T(8,128)(2,1)} %grad_h.1, bf16[1792,4096]{1,0:T(8,128)(2,1)} %down_h.1, bf16[64,2048]{1,0:T(8,128)(2,1)} %bitcast.2, bf16[64,1792]{1,0:T(8,128)(2,1)} %bitcast.3, f32[64,64]{1,0:T(8,128)} %cin_h.1, ...), custom_call_target="tpu_custom_call" | custom-call | flops 7516192768 | bytes 14680064 | tf_op jit(solution)/shard_map/pallas_call | solution.py:268
  23.9 1.2 %copy.11 = f32[1,64]{1,0:T(1,128)} copy(f32[1,64]{1,0:T(1,128)} %shard_map.91) | data formatting | bytes 512

commit v3 on v2

--- a/solution.py
+++ b/solution.py
@@ -29,9 +29,7 @@
     down_sem, load_sem,
     grad_sem, left_send, left_recv, q_send, q_recv, qc_send, qc_recv, s_send, s_recv,
 ):
-    groups, dp, tensor, seq, chunk = dims
-    ff = down.shape[0]
-    chunks = ff // chunk
+    groups, dp, tensor, seq, first, second = dims
     tokens = grad.shape[1]
     k1 = cin.shape[0]
     nq_block = query.shape[0]
@@ -55,32 +53,28 @@
     for k in range(1, dp):
         pl.semaphore_signal(barrier, inc=1, device_id=along(k), device_id_type=MESH)
 
-    def rows_of(c):
-        return pl.ds(pl.multiple_of(c * chunk, chunk), chunk)
-
     def load(src, dst, i):
         copy = pltpu.make_async_copy(src, dst, load_sem.at[i])
         copy.start()
         return copy
 
     def down_copy(c):
-        return pltpu.make_async_copy(
-            down_h.at[rows_of(c)], down.at[rows_of(c)], down_sem.at[c]
-        )
+        rows = pl.ds(*first[c])
+        return pltpu.make_async_copy(down_h.at[rows], down.at[rows], down_sem.at[c])
 
     def token_rows(b):
         return pl.ds(pl.multiple_of(b * tokens, tokens), tokens)
 
+    get_query = load(query_h, query, 0)
     get_act = load(act_h.at[0], act, 1)
     get_pin = load(pin_h, pin, 2)
-    get_query = load(query_h, query, 0)
     get_cin = load(cin_h, cin, 3)
     get_cout = load(cout_h, cout, 4)
     get_pout = load(pout_h, pout, 5)
     get_grad = load(grad_h.at[0], grad.at[0], 6)
     down_copy(0).start()
     get_gate0 = load(gate_h.at[0, token_rows(s)], gate.at[0], 7)
-    for c in range(1, chunks):
+    for c in range(1, len(first)):
         down_copy(c).start()
     get_gate1 = load(gate_h.at[0, token_rows(other)], gate.at[1], 8)
 
@@ -125,9 +119,6 @@
             device_id=peer(k), device_id_type=MESH,
         )
 
-    for k in range(1, ranks):
-        left_copy(k, me).start()
-
     get_cout.wait()
     get_pout.wait()
     k2 = cout.shape[0]
@@ -135,8 +126,11 @@
     y = lax.dot_general(cout2, pout[...], NN, preferred_element_type=F32)
     pout2 = jnp.concatenate(split(y[:k2] + y[k2:]), axis=0)
 
-    def step(phase, c):
-        rows = slice(c * chunk, (c + 1) * chunk)
+    for k in range(1, ranks):
+        left_copy(k, me).start()
+
+    def step(phase, start, size):
+        rows = slice(start, start + size)
         hid = lax.dot_general(down[rows, :], grad[phase], NT, preferred_element_type=F32)
         v = gate[phase, :, rows].astype(F32).T
         up = (hid * (v / (1.0 + jnp.exp(-v)))).astype(BF16)
@@ -145,9 +139,9 @@
     get_grad.wait()
     get_gate0.wait()
     right0 = 0.0
-    for c in range(chunks):
+    for c in range(len(first)):
         down_copy(c).wait()
-        right0 = right0 + step(0, c)
+        right0 = right0 + step(0, *first[c])
 
     get_gate1.wait()
     send_grad.wait()
@@ -177,8 +171,8 @@
 
     m = product(right0, s)
     right1 = 0.0
-    for c in range(chunks):
-        right1 = right1 + step(1, c)
+    for piece in second:
+        right1 = right1 + step(1, *piece)
     m = m + product(right1, other)
     m = m[:k1] + m[k1:]
     m = m[:, :2 * k2] + m[:, 2 * k2:]
@@ -227,6 +221,17 @@
         qc_copy(lax.rem(z + dp - k, dp), s).wait_send()
 
 
+def pieces(total, sizes):
+    out, start = [], 0
+    for i in range(total):
+        if start == total:
+            break
+        size = min(sizes[min(i, len(sizes) - 1)], total - start)
+        out.append((start, size))
+        start += size
+    return tuple(out)
+
+
 def solution(mesh):
     shape = dict(mesh.shape)
     groups, dp, tensor, seq = (shape[a] for a in ("groups", "dp", "tensor", "seq"))
@@ -238,8 +243,7 @@
         pin, pout = pin.T, pout.T
         k1, k2 = pin.shape[0], pout.shape[0]
         nq_block, width = query.shape
-        chunk = next(c for c in (896, 512, 256, 128) if ff % c == 0)
-        chunks = ff // chunk
+        first, second = pieces(ff, (512, 512, 768)), pieces(ff, (1024, 768))
         ranks = tensor * seq
         nq = nq_block * dp
         scale = 1.0 / math.sqrt(gate.shape[1] * k1 * k2)
@@ -257,7 +261,7 @@
             pltpu.VMEM((dp, seq, nq_block, width // seq), BF16),
             pltpu.VMEM((ranks, k1, tokens), F32),
             pltpu.VMEM((ranks, 8, nq), F32),
-            dma((chunks,)),
+            dma((len(first),)),
             dma((9,)),
             dma((2,)),
             dma((ranks,)), dma((ranks,)),
@@ -266,7 +270,7 @@
             dma((ranks,)), dma((ranks,)),
         ]
         return pl.pallas_call(
-            functools.partial(kernel, (groups, dp, tensor, seq, chunk), scale),
+            functools.partial(kernel, (groups, dp, tensor, seq, first, second), scale),
             out_shape=jax.ShapeDtypeStruct((1, nq), F32),
             in_specs=[pl.BlockSpec(memory_space=pl.ANY)] * 9,
             out_specs=pl.BlockSpec(memory_space=pltpu.VMEM),

time: 25.2 us -> 24.7 us (0.980)
  Pallas kernels: 23.9 us -> 23.3 us
    pallas_call x1, Pallas kernels: 23.9 us -> 23.3 us  [body(): pl.pallas_call(functools.partial(kernel, (groups, dp, tensor, seq, first,...]
where the time goes in v3:
time: 24.7 us; the launch traced here: 24.5 us
  Pallas kernels  23.3 us (94%)
  local copies, waits for them, and re-layouts  1.19 us (5%)
    pallas_call x1, Pallas kernels, body(): pl.pallas_call(functools.partial(kernel, (groups, dp, tensor, seq, first,...  23.3 us
    unnamed x1, local copies, waits for them, and re-layouts  1.19 us

profile of v3, /device:TPU:0, one launch (start us, length us, event | category | flops | bytes accessed | tf_op | source)
XLA Modules:
  0.0 24.5 jit_solution(283073717358002414)
XLA Ops:
  0.0 23.3 %shard_map.91 = f32[1,64]{1,0:T(1,128)} custom-call(bf16[1,256,2048]{2,1,0:T(8,128)(2,1)} %act_h.1, bf16[1,512,1792]{2,1,0:T(8,128)(2,1)} %gate_h.1, bf16[1,256,4096]{2,1,0:T(8,128)(2,1)} %grad_h.1, bf16[1792,4096]{1,0:T(8,128)(2,1)} %down_h.1, bf16[64,2048]{1,0:T(8,128)(2,1)} %bitcast.2, bf16[64,1792]{1,0:T(8,128)(2,1)} %bitcast.3, f32[64,64]{1,0:T(8,128)} %cin_h.1, ...), custom_call_target="tpu_custom_call" | custom-call | flops 7516192768 | bytes 14680064 | tf_op jit(solution)/shard_map/pallas_call | solution.py:272
  23.3 1.2 %copy.11 = f32[1,64]{1,0:T(1,128)} copy(f32[1,64]{1,0:T(1,128)} %shard_map.91) | data formatting | bytes 512
